TPU v7x, 32 devices: a whole 2x2x4 slice. The times are simulated.
32 devices in a mesh: groups: 2 (over y), chan: 4 (over z), win: 2 (over x), sub: 2 (over core).
Axes of the slice: x: 2, y: 2, z: 4, core: 2. Of those that a mesh axis runs over, the one named last changes fastest.
Arguments:
- traces: bfloat16 [4, 2560, 1024], P(('groups', 'win'), 'chan'), parts along dimension 0, may hold values from -240 to 240, as said below
- channel_mask: int32 [5120], P(('groups', 'chan')), parts along dimension 0, may hold values 0 or 1
- smooth_width: int32 [512], replicated, may hold values from 1 to 16, as said below
- source_phase: int32 [8], P('groups'), parts along dimension 0, may hold values from 0 to 7
- pair_list: int32 [8, 5], P('groups'), parts along dimension 0, may hold values 0 or 1
Outputs:
- receiver_stack: float32 [8, 5, 101, 5120], P(('win', 'sub'), None, None, ('groups', 'chan')), parts along dimension 3
- source_stack: float32 [64, 5, 101, 640], P(('groups', 'chan', 'win', 'sub')), parts along dimension 0
There are 2 independent parts, one for each index of `groups`. A program takes and returns all parts, laid end to end along the dimension named above; an argument that names none is the same for every part. Nothing has to cross between parts.
Inputs may be any that keep to these rules, and one draw needn't show every extreme that they name: `traces`: float samples; each channel and each window has a scale of its own. `smooth_width`: every value from 1 to 16 may occur; 16 occurs in every draw.
All inputs are finite; a program needn't handle non-finite values. No bound on the sum of `channel_mask` on one device may be relied on, other than what follows from the above.
Results may differ from a plain program's by a relative error of at most 0.0052.
Values may be sent and summed in bfloat16 or wider, within the bound.
No kernel may reach another device: no remote copies, remote signals or barrier semaphores. Data moves between devices by JAX's collectives and lax.ppermute only.
A program may use at most 192 MiB of HBM per device.

v0:
```python
import functools
import math

import jax
import jax.numpy as jnp
import numpy as np
from jax import lax
from jax.experimental import pallas as pl
from jax.experimental.pallas import tpu as pltpu
from jax.sharding import PartitionSpec as P

NB = 512
MAXLAG = 50
STRIDE = 8
REACH = 2
VS = 8
OFFS = 5
LAGS = 2 * MAXLAG + 1
FLOOR = 0.25
TABLE_PARTS = 4
LANES = 128
VMEM = pl.BlockSpec(memory_space=pltpu.VMEM)
SMEM = pl.BlockSpec(memory_space=pltpu.SMEM)
HBM = pl.BlockSpec(memory_space=pltpu.HBM)
NT = (((1,), (1,)), ((), ()))


def dft_table(samples):
    phases = np.arange(samples)[:, None] * np.arange(NB)[None, :] % samples
    angles = phases * (2.0 * math.pi / samples)
    table = np.concatenate([np.cos(angles), -np.sin(angles)], axis=1)
    return jnp.asarray(table.astype(np.float32), jnp.bfloat16)


def side_rows(per_device):
    return -(-(MAXLAG + 1) * per_device // 8) * 8


def lag_row(tau, per_device):
    return abs(tau) * per_device + (0 if tau >= 0 else side_rows(per_device))


def lag_table(samples, per_device):
    lag = np.arange(side_rows(per_device)) // per_device
    angles = (lag[:, None] * np.arange(NB)[None, :] % samples) * (2.0 * math.pi / samples)
    table = np.concatenate([np.cos(angles), np.sin(angles)], axis=1)
    return jnp.asarray(table, jnp.float32)


def params(mib):
    return pltpu.CompilerParams(vmem_limit_bytes=mib << 20)


def cost(flops, moved):
    return pl.CostEstimate(flops=flops, bytes_accessed=moved, transcendentals=0)


SHORT, LONG = cost(1 << 20, 1 << 18), cost(1 << 33, 1 << 26)


def whiten(rows, table, weights, share):
    samples = rows.shape[1]
    spectrum = jnp.dot(rows, table, preferred_element_type=jnp.float32) * samples ** (-0.5)
    real, imag = spectrum[:, :NB], spectrum[:, NB:]
    amplitude = jnp.sqrt(real * real + imag * imag)
    high = amplitude.astype(jnp.bfloat16)
    low = (amplitude - high.astype(jnp.float32)).astype(jnp.bfloat16)
    total = jnp.dot(high, weights, preferred_element_type=jnp.float32)
    total += jnp.dot(low, weights, preferred_element_type=jnp.float32)
    gain = 1.0 / jnp.maximum(total * share, FLOOR)
    return (real * gain).astype(jnp.bfloat16), (imag * gain).astype(jnp.bfloat16)


def near_kernel(layout, phases, mask, *refs):
    windows, subs, per_device = layout
    halves, out = refs[:-1], refs[-1]
    block_at, win_at, sub_at = lax.axis_index("chan"), lax.axis_index("win"), lax.axis_index("sub")
    group = per_device * STRIDE
    rows, width = out.shape[0], halves[0].shape[0]
    phase = phases[block_at]

    def ones_at(first, width):
        row = lax.broadcasted_iota(jnp.int32, (rows, width), 0)
        place = lax.broadcasted_iota(jnp.int32, (rows, width), 1)
        return row, place == first + phase + STRIDE * (row % per_device)

    row, here = ones_at((win_at * subs + sub_at) * group, mask.shape[1])
    alive = jnp.sum(jnp.where(here, mask[...].astype(jnp.float32), 0.0), axis=1, keepdims=True)
    row, here = ones_at(win_at * group, width)
    total = jnp.zeros(out.shape, jnp.float32)
    for behind in range(windows):
        chosen = jnp.where(here & (row // per_device == behind), 1.0, 0.0).astype(jnp.bfloat16)
        total += jnp.dot(chosen, halves[behind][...], preferred_element_type=jnp.float32)
    out[...] = total * alive


def setup_kernel(chunks, traces, table, widths, *refs):
    owns, (weights, share, rows_kept, table_kept, sems, *scratch) = refs[:len(chunks)], refs[len(chunks):]
    depth = table.shape[0] // TABLE_PARTS
    needed = chunks[-1][0] + chunks[-1][1]
    rest = rows_kept.shape[0] - needed
    first_rows = pltpu.make_async_copy(traces.at[0, pl.ds(0, needed)], rows_kept.at[pl.ds(0, needed)], sems.at[TABLE_PARTS])
    first_rows.start()
    parts = []
    for i in range(TABLE_PARTS):
        span = pl.ds(i * depth, depth)
        parts.append(pltpu.make_async_copy(table.at[span], table_kept.at[span], sems.at[i]))
        parts[-1].start()
    if rest:
        span = pl.ds(needed, rest)
        last_rows = pltpu.make_async_copy(traces.at[0, span], rows_kept.at[span], sems.at[TABLE_PARTS + 1])
        last_rows.start()
    widths_kept, = scratch
    fetched = pltpu.make_async_copy(widths, widths_kept, sems.at[TABLE_PARTS + 2])
    fetched.start()
    fetched.wait()
    reach = widths_kept[...]
    near = lax.broadcasted_iota(jnp.int32, (NB, NB), 0)
    here = lax.broadcasted_iota(jnp.int32, (NB, NB), 1)
    weights[...] = jnp.where(jnp.abs(near - here) <= reach, 1.0, 0.0).astype(jnp.bfloat16)
    bins = lax.broadcasted_iota(jnp.int32, (1, NB), 1)
    count = jnp.minimum(bins + reach, NB - 1) - jnp.maximum(bins - reach, 0) + 1
    share[...] = 1.0 / count.astype(jnp.float32)
    first_rows.wait()
    for part in parts:
        part.wait()
    for (start, size), own in zip(chunks, owns):
        own_kernel(start, rows_kept, table_kept, weights, share, own)
    if rest:
        last_rows.wait()


def own_kernel(start, rows, table, weights, share, out):
    real, imag = whiten(rows[start:start + out.shape[0], :], table[...], weights[...], share[...])
    out[:, :NB] = real
    out[:, NB:] = imag


def turn_kernel(layout, table, weights, share, lags, *refs):
    per_device, windows, places = layout
    even = lax.axis_index("sub") % 2 == 0
    picked, turned, spectra = refs[:-2], refs[-2], refs[-1]
    rows = jnp.concatenate([p[...].astype(jnp.float32) for p in picked], axis=0).astype(jnp.bfloat16)
    real, imag = whiten(rows, table[...], weights[...], share[...])
    spectra[:, :NB] = real.astype(jnp.float32)
    spectra[:, NB:] = imag.astype(jnp.float32)
    side = side_rows(per_device)
    span = 2 * side
    which = lax.broadcasted_iota(jnp.int32, (8, LANES), 0) % per_device

    def rows_of(first, lane):
        tiled = jnp.zeros((8, LANES), jnp.float32)
        for v in range(per_device):
            rows = [spectra[f + v:f + v + 1, lane:lane + LANES] for f in first]
            row = rows[0] if first[0] == first[-1] else jnp.where(even, rows[0], rows[-1])
            tiled = jnp.where(which == v, row, tiled)
        return tiled[None]

    for lane in range(0, NB, LANES):
        cosine = lags[:, lane:lane + LANES].reshape(side // 8, 8, LANES)
        sine = lags[:, NB + lane:NB + lane + LANES].reshape(side // 8, 8, LANES)
        for at, place in enumerate(places):
            for behind in range(windows):
                first = [(here * windows + behind) * per_device for here in place]
                real, imag = rows_of(first, lane), rows_of(first, NB + lane)
                cr, si, sr, ci = cosine * real, sine * imag, sine * real, cosine * imag
                up = jnp.concatenate([cr - si, cr + si], axis=0).reshape(span, LANES)
                down = jnp.concatenate([ci + sr, ci - sr], axis=0).reshape(span, LANES)
                spot = pl.ds(at * span, span)
                turned[behind, spot, lane:lane + LANES] = up.astype(jnp.bfloat16)
                turned[behind, spot, NB + lane:NB + lane + LANES] = down.astype(jnp.bfloat16)


def others_kernel(table, weights, share, *refs):
    parts, (white, raw) = refs[:-2], refs[-2:]
    sub_at = lax.axis_index("sub")
    groups, _, group, samples = raw.shape
    each = len(parts) // white.shape[0]
    for i in range(white.shape[0]):
        if each == 1:
            rows = parts[i][...]
        else:
            for half, place in ((parts[2 * i], sub_at), (parts[2 * i + 1], 1 - sub_at)):
                raw[:, pl.ds(place, 1)] = half[...].reshape(groups, 1, group, samples)
            rows = raw[...].reshape(white.shape[1], samples)
        real, imag = whiten(rows, table[...], weights[...], share[...])
        white[i, :, :NB] = real
        white[i, :, NB:] = imag


def lag_product(turned, own, white):
    total = lax.dot_general(turned[0], own[...], NT, preferred_element_type=jnp.float32)
    for i in range(white.shape[0]):
        total += lax.dot_general(turned[1 + i], white[i], NT, preferred_element_type=jnp.float32)
    return total


def base_kernel(turned, own, base):
    base[...] = lax.dot_general(turned[0], own[...], NT, preferred_element_type=jnp.float32)


def lag_kernel(factor, based, turned, own, white, mask, *pieces):
    if based:
        total = own[...]
        for i in range(white.shape[0]):
            total += lax.dot_general(turned[1 + i], white[i], NT, preferred_element_type=jnp.float32)
    else:
        total = lag_product(turned, own, white)
    result = total * (mask[...].astype(jnp.float32) * factor)
    span = result.shape[0] // len(pieces)
    for at, piece in enumerate(pieces):
        piece[...] = result[at * span:(at + 1) * span, :].astype(jnp.bfloat16)


def first_kernel(layout, factor, count, table, weights, share, lags, own, white, mask, *refs):
    sources, (turned, *pieces, spectra) = refs[:count], refs[count:]
    turn_kernel(layout, table, weights, share, lags, *sources, turned, spectra)
    lag_kernel(factor, False, turned, own, white, mask, *pieces)


def put_slots(layout, listed, wide, out, stage, sems, slot):
    tie, blocks, per_device, first, reverse = layout
    block_at, tie = lax.axis_index("chan"), on_core(tie, lax.axis_index("sub"))
    row = lax.broadcasted_iota(jnp.int32, listed.shape, 0)
    column = lax.broadcasted_iota(jnp.int32, listed.shape, 1)
    width = stage.shape[3]
    block = block_at if reverse else partner(block_at, blocks, tie)
    copies = []
    for e in offsets_of(block_at, blocks, tie, reverse):
        chosen = jnp.where((row == block) & (column == e), listed, 0.0)
        pair = jnp.broadcast_to(jnp.sum(chosen, keepdims=True), (per_device, width))
        for t in range(LAGS):
            tau = MAXLAG - t if reverse else t - MAXLAG
            spot = lag_row(tau, per_device)
            stage[slot, t] = wide[spot:spot + per_device, :] * pair
        target = out.at[e, :, :, pl.ds(first, width)]
        copies.append(pltpu.make_async_copy(stage.at[slot], target, sems.at[slot]))
        copies[-1].start()
        slot += 1
    return copies


def receiver_kernel(layout, pairs, turned, mask, *refs):
    ties, blocks, per_device, chunks, factor = layout
    count = len(chunks)
    owns, whites, pieces = refs[:count], refs[count:2 * count], refs[2 * count:-5]
    out, source_out, wide, stage, sems = refs[-5:]
    listed = pairs[...].astype(jnp.float32)
    copies = []
    for at, tie in enumerate(ties):
        for i, (start, size) in enumerate(chunks):
            lanes = slice(start, start + size)
            if at:
                wide[at, :, lanes] = pieces[i * (len(ties) - 1) + at - 1][...].astype(jnp.float32)
            else:
                wide[at, :, lanes] = lag_product(turned, owns[i], whites[i]) * (mask[:, lanes].astype(jnp.float32) * factor)
        turns = [(out, False)] + ([] if at else [(source_out, True)])
        for target, reverse in turns:
            part = (tie, blocks, per_device, 0, reverse)
            copies += put_slots(part, listed, wide.at[at], target, stage, sems, len(copies))
    for copy in copies:
        copy.wait()


def source_kernel(layout, pairs, *refs):
    ties, blocks, per_device, first = layout
    pieces, (_, out, wide, stage, sems) = refs[:len(ties)], refs[len(ties):]
    listed = pairs[...].astype(jnp.float32)
    copies = []
    for at, tie in enumerate(ties):
        wide[at] = pieces[at][...].astype(jnp.float32)
        part = (tie, blocks, per_device, first, True)
        copies += put_slots(part, listed, wide.at[at], out, stage, sems, len(copies))
    for copy in copies:
        copy.wait()


def ties_of(blocks, subs):
    if blocks == 4:
        return [("xor", (step,) * subs) for step in (0, 2, 3, 1)]
    ties = []
    for moved in (0, 1, -1, 2, -2):
        if all((m[0] - moved) % blocks for _, m in ties):
            ties.append(("shift", (moved,) * subs))
    return ties


def on_core(tie, core):
    kind, steps = tie
    if len(set(steps)) == 1:
        return kind, steps[0]
    return kind, jnp.where(core % 2 == 0, steps[0], steps[1])


def partner(block, blocks, tie, back=False):
    kind, step = tie
    if kind == "xor":
        return block ^ step
    return (block + (step if back else -step) + blocks) % blocks


def offsets_of(block, blocks, tie, back):
    kind, step = tie
    if kind == "shift":
        return [e for e in range(OFFS) if (e - REACH - step) % blocks == 0]
    if isinstance(step, int) and step % 2 == 0:
        return [e for e in range(OFFS) if abs(e - REACH) == step]
    ahead = (block ^ step) - block if back else block - (block ^ step)
    return [jnp.where((ahead + blocks) % blocks == 1, REACH + 1, REACH - 1)]


def exchange(value, blocks, subs, tie, back=False):
    kind, steps = tie
    route = [
        (partner(b, blocks, (kind, steps[c]), back) * subs + c, b * subs + c)
        for b in range(blocks)
        for c in range(subs)
    ]
    return lax.ppermute(value, ("chan", "sub"), route)


def chunks_of(channels):
    if channels < 2 * LANES or channels % LANES:
        return [(0, channels)]
    first = channels * 2 // 5 // LANES * LANES
    return [(0, first), (first, channels - first)]


def shift(block, axis, distance):
    count = lax.axis_size(axis)
    return lax.ppermute(block, axis, [(i, (i + distance) % count) for i in range(count)])


def slots_of(ties, blocks):
    return sum(len(offsets_of(0, blocks, (kind, steps[0]), False)) for kind, steps in ties)


def in_hbm(value):
    return pltpu.with_memory_space_constraint(value, pltpu.HBM)


def after(value, *others):
    return lax.optimization_barrier((value, *others))[0]


def on_device(traces, channel_mask, smooth_width, source_phase, pair_list):
    _, channels, samples = traces.shape
    blocks, windows, subs = (lax.axis_size(a) for a in ("chan", "win", "sub"))
    sub_at = lax.axis_index("sub")
    per_device = VS // (windows * subs)
    group = per_device * STRIDE
    ties = ties_of(blocks, subs)
    span = 2 * side_rows(per_device)
    chunks = chunks_of(channels)
    table, lags = dft_table(samples), lag_table(samples, per_device)
    factor = (NB * windows) ** (-0.5)
    bf16, f32 = jnp.bfloat16, jnp.float32
    like = jax.ShapeDtypeStruct
    mask_row = channel_mask.reshape(1, channels)

    def half_of(rows, start, size):
        grouped = rows.reshape(channels // (subs * group), subs, group, samples)
        first, count = start // (subs * group), size // (subs * group)
        half = lax.dynamic_slice(grouped, (first, sub_at, 0, 0), (count, 1, group, samples))
        return half.reshape(size // subs, samples)

    def from_windows(half):
        return [shift(half, "win", d) for d in range(1, windows)]

    def with_other_core(received):
        return [side for piece in received for side in (piece, shift(piece, "sub", 1))]

    def whiten_others(size, both, hint):
        return pl.pallas_call(
            others_kernel,
            out_shape=like((windows - 1, size, 2 * NB), bf16),
            in_specs=[VMEM] * (3 + len(both)),
            out_specs=VMEM,
            scratch_shapes=[pltpu.VMEM((size // (subs * group), subs, group, samples), bf16)],
            compiler_params=params(24),
            cost_estimate=hint,
            name="whiten_others",
        )(table, weights, share, *both)

    def correlate(start, size, turned, base, white):
        count = turned.shape[1] // span
        return pl.pallas_call(
            functools.partial(lag_kernel, factor, True),
            out_shape=tuple(like((span, size), bf16) for _ in range(count)),
            in_specs=[VMEM] * 4,
            out_specs=(VMEM,) * count,
            compiler_params=params(24),
            cost_estimate=LONG,
            name="lag_pieces",
        )(turned, base, white, mask_row[:, start:start + size])

    half = half_of(traces, *chunks[0])
    received = [from_windows(half)]
    *owns, weights, share, rows, table = pl.pallas_call(
        functools.partial(setup_kernel, chunks),
        out_shape=tuple(like((size, 2 * NB), bf16) for _, size in chunks)
        + (like((NB, NB), bf16), like((1, NB), f32))
        + (like((channels, samples), bf16), like(table.shape, bf16)),
        in_specs=[HBM, HBM, HBM],
        out_specs=(VMEM,) * (len(chunks) + 4),
        scratch_shapes=[pltpu.SemaphoreType.DMA((TABLE_PARTS + 3,)), pltpu.VMEM((1, NB), jnp.int32)],
        compiler_params=params(24),
        cost_estimate=SHORT,
        name="whiten_own",
    )(in_hbm(traces), in_hbm(table), in_hbm(after(smooth_width, half).reshape(1, NB)))
    received += [from_windows(after(rows, share)[a:a + n]) for a, n in chunks[1:]]
    near = pl.pallas_call(
        functools.partial(near_kernel, (windows, subs, per_device)),
        out_shape=like((windows * per_device, samples), f32),
        in_specs=[SMEM] + [VMEM] * (1 + windows),
        out_specs=VMEM,
        compiler_params=params(16),
        cost_estimate=SHORT,
        name="pick_sources",
    )(source_phase, after(mask_row, weights), half, *received[0])

    def turn(sources, places, hint, *first):
        rows_each = windows * per_device
        return pl.pallas_call(
            functools.partial(turn_kernel, (per_device, windows, places)),
            out_shape=like((windows, len(places) * span, 2 * NB), bf16),
            in_specs=[VMEM] * (4 + len(sources)),
            out_specs=VMEM,
            scratch_shapes=[pltpu.VMEM((len(places) * rows_each, 2 * NB), f32)],
            compiler_params=params(24),
            cost_estimate=hint,
            name="turn_sources",
        )(table, weights, after(share, *first), lags, *sources)

    turned_own = turn([near], [(0,)], LONG)
    inbound = with_other_core(received[0])
    white = whiten_others(chunks[0][1], inbound, SHORT)
    if ties[1][0] == "xor":
        beside = exchange(near, blocks, subs, ("xor", (1,) * subs))
        two = jnp.concatenate([after(near, turned_own), beside], axis=0).astype(bf16)
        sources = [beside, exchange(two, blocks, subs, ("xor", (2,) * subs))]
        places = [tuple(step - 1 for step in steps) for _, steps in ties[1:]]
    else:
        sources = [exchange(near, blocks, subs, tie) for tie in ties[1:]]
        places = [(at,) for at in range(len(sources))]
    start, size = chunks[0]
    count = len(places)
    turned, *first_pieces = pl.pallas_call(
        functools.partial(first_kernel, (per_device, windows, places), factor, len(sources)),
        out_shape=(like((windows, count * span, 2 * NB), bf16),) + (like((span, size), bf16),) * count,
        in_specs=[VMEM] * (7 + len(sources)),
        out_specs=(VMEM,) * (1 + count),
        scratch_shapes=[pltpu.VMEM((count * windows * per_device, 2 * NB), f32)],
        compiler_params=params(24),
        cost_estimate=SHORT,
        name="turn_and_lag",
    )(table, weights, share, lags, owns[0], white, mask_row[:, start:start + size], *sources)
    pieces, arrived, whites = [], [], [white]
    for i, (start, size) in enumerate(chunks):
        if i:
            whites.append(whiten_others(size, [after(r, *pieces[-1]) for r in received[i]], LONG))
            base = pl.pallas_call(
                base_kernel,
                out_shape=like((turned.shape[1], size), f32),
                in_specs=[VMEM, VMEM],
                out_specs=VMEM,
                compiler_params=params(24),
                cost_estimate=SHORT,
                name="lag_base",
            )(after(turned, *pieces[-1]), owns[i])
            pieces.append(correlate(start, size, turned, base, whites[i]))
        else:
            pieces.append(tuple(first_pieces))
        ahead = arrived[-1][:1] if i else []
        sent = [after(p, *ahead) for p in pieces[-1]]
        arrived.append([exchange(p, blocks, subs, tie, True) for tie, p in zip(ties[1:], sent)])
    stack = like((OFFS, LAGS, per_device, channels), f32)

    def scratch(count, slots, width):
        return [
            pltpu.VMEM((count, span, width), f32),
            pltpu.VMEM((slots, LAGS, per_device, width), f32),
            pltpu.SemaphoreType.DMA((slots,)),
        ]

    remote = [piece for group in pieces for piece in group]
    receiver_stack, source_stack = pl.pallas_call(
        functools.partial(receiver_kernel, (ties, blocks, per_device, chunks, factor)),
        out_shape=(stack, stack),
        in_specs=[VMEM] * (3 + 2 * len(chunks) + len(remote)),
        out_specs=(HBM, HBM),
        scratch_shapes=scratch(len(ties), slots_of(ties, blocks) + 1, channels),
        compiler_params=params(24),
        cost_estimate=LONG,
        name="receiver_order",
    )(pair_list, turned_own, mask_row, *owns, *whites, *remote)
    slots = slots_of(ties[1:], blocks)
    for (start, size), back in zip(chunks, arrived):
        source_stack = pl.pallas_call(
            functools.partial(source_kernel, (ties[1:], blocks, per_device, start)),
            out_shape=stack,
            in_specs=[VMEM] * (1 + count) + [HBM],
            out_specs=HBM,
            scratch_shapes=scratch(count, slots, size),
            input_output_aliases={1 + count: 0},
            compiler_params=params(16),
            cost_estimate=SHORT,
            name="source_order",
        )(pair_list, *back, source_stack)
    order = (2, 0, 1, 3)
    return (jnp.transpose(receiver_stack, order), jnp.transpose(source_stack, order))


def solution(mesh):
    in_specs = (
        P(("groups", "win"), "chan", None),
        P(("groups", "chan")),
        P(),
        P("groups"),
        P("groups", None),
    )
    out_specs = (
        P(("win", "sub"), None, None, ("groups", "chan")),
        P(("groups", "chan", "win", "sub"), None, None, None),
    )
    return jax.shard_map(
        on_device, mesh=mesh, in_specs=in_specs, out_specs=out_specs, check_vma=False
    )
```

profile of v0, /device:TPU:17, one launch (start us, length us, event | category | flops | bytes accessed | tf_op | source)
XLA Modules:
  0.0 47.1 jit_solution(7812946441919603370)
XLA Ops:
  0.6 1.0 %constant_dynamic-slice_fusion = bf16[8,1,16,1024]{3,2,1,0:T(8,128)(2,1)S(1)} fusion(bf16[20,2,16,1024]{3,2,1,0:T(8,128)(2,1)} %bitcast.10, s32[]{:T(128)S(6)} %select_n.3), kind=kLoop, calls=%fused_computation.1 | loop fusion | bytes 524292 | tf_op jit(solution)/shard_map/dynamic_slice | solution.py:364
  1.6 0.0 copy-start.3
  1.6 0.0 copy-start.2
  1.6 1.3 %collective-permute-start = (bf16[128,1024]{1,0:T(8,128)(2,1)S(1)}, bf16[128,1024]{1,0:T(8,128)(2,1)S(1)}, u32[]{:S(2)}, u32[]{:S(2)}) collective-permute-start(bf16[128,1024]{1,0:T(8,128)(2,1)S(1)} %bitcast.7), channel_id=1, source_target_pairs={{0,2},{2,0},{1,3},{3,1},{4,6},{6,4},{5,7},{7,5},{8,10},{10,8},{9,1... | collective-permute-start | bytes 786440 | tf_op jit(solution)/shard_map/ppermute | solution.py:331
  2.9 0.0 copy-start
  2.9 4.8 %whiten_own.1 = (bf16[256,1024]{1,0:T(8,128)(2,1)S(1)}, bf16[384,1024]{1,0:T(8,128)(2,1)S(1)}, bf16[512,512]{1,0:T(8,128)(2,1)S(1)}, f32[1,512]{1,0:T(1,128)S(1)...) custom-call(bf16[1,640,1024]{2,1,0:T(8,128)(2,1)} %traces.1, bf16[1024,1024]{1,0:T(8,128)(2,1)} %constant.12.clone.table, ...), custom_call_target="tpu_custom_call" | custom-call | flops 1048576 | bytes 262144 | tf_op jit(solution)/shard_map/whiten_own/pallas_call | solution.py:399
  7.7 0.1 slice.9
  7.8 0.3 collective-permute-start.2
  8.1 0.0 copy-done.3
  8.1 0.8 %collective-permute-done.refs_1_.refs_0_ = bf16[128,1024]{1,0:T(8,128)(2,1)S(1)} collective-permute-done((bf16[128,1024]{1,0:T(8,128)(2,1)S(1)}, bf16[128,1024]{1,0:T(8,128)(2,1)S(1)}, u32[]{:S(2)}, u32[]{:S(2)}) %collective-permute-start) | collective-permute-done | bytes 262176 | tf_op jit(solution)/shard_map/ppermute | solution.py:331
  8.9 0.0 copy-done.2
  8.9 0.7 %pick_sources.1.refs_0_ = f32[4,1024]{1,0:T(4,128)S(1)} custom-call(s32[4]{0:T(128)S(1)} %copy-done.2, s32[1,640]{1,0:T(1,128)S(1)} %reshape.19.mask, bf16[128,1024]{1,0:T(8,128)(2,1)S(1)} %bitcast.8, bf16[128,1024]{1,0:T(8,128)(2,1)S(1)} %collective-permute-done.refs_1_.refs_0_), custom_call_target="tpu_custom_call" | custom-call | flops 1048576 | bytes 262144 | tf_op jit(solution)/shard_map/pick_sources/pallas_call | solution.py:412
  9.6 1.3 %collective-permute-start.3 = (f32[4,1024]{1,0:T(4,128)S(1)}, f32[4,1024]{1,0:T(4,128)S(1)}, u32[]{:S(2)}, u32[]{:S(2)}) collective-permute-start(f32[4,1024]{1,0:T(4,128)S(1)} %pick_sources.1.refs_0_), channel_id=1, source_target_pairs={{4,0},{5,1},{0,4},{1,5},{12,8},{13,9},{8,12},{9,13},{6,2},{7,3},{2... | collective-permute-start | bytes 49160 | tf_op jit(solution)/shard_map/ppermute | solution.py:319
  10.9 1.8 %collective-permute-start.1 = (bf16[128,1024]{1,0:T(8,128)(2,1)S(1)}, bf16[128,1024]{1,0:T(8,128)(2,1)S(1)}, u32[]{:S(2)}, u32[]{:S(2)}) collective-permute-start(bf16[128,1024]{1,0:T(8,128)(2,1)S(1)} %collective-permute-done.refs_1_.refs_0_), channel_id=1, source_target_pairs={{0,1},{1,0},{2,3},{3,2},{4,5},{5,4},{6,7},{7,6},{8,9},{9,8},{10,11... | collective-permute-start | bytes 786440 | tf_op jit(solution)/shard_map/ppermute | solution.py:331
  12.7 0.0 copy-done
  12.7 0.9 %turn_sources.1.turned = bf16[2,208,1024]{2,1,0:T(8,128)(2,1)S(1)} custom-call(bf16[1024,1024]{1,0:T(8,128)(2,1)S(1)} %get-tuple-element.27.table, bf16[512,512]{1,0:T(8,128)(2,1)S(1)} %get-tuple-element.28.weights, f32[1,512]{1,0:T(1,128)S(1)} %get-tuple-element.29.share, f32[104,1024]{1,0:T(8,128)S(1)} %copy-done, f32[4,1024]{1,0:T(4,128)S(1)} %pick_sources.1.refs_0_), custom_call_target="tpu_custom_call" | custom-call | flops 8589934592 | bytes 67108864 | tf_op jit(solution)/shard_map/turn_sources/pallas_call | solution.py:424
  13.7 0.0 collective-permute-done.3.refs_0_
  13.7 0.1 collective-permute-start.4
  13.9 0.0 collective-permute-done.1.refs_1_
  13.9 1.2 %whiten_others.2.white.refs_2_ = bf16[1,256,1024]{2,1,0:T(8,128)(2,1)S(1)} custom-call(bf16[1024,1024]{1,0:T(8,128)(2,1)S(1)} %get-tuple-element.27.table, bf16[512,512]{1,0:T(8,128)(2,1)S(1)} %get-tuple-element.28.weights, f32[1,512]{1,0:T(1,128)S(1)} %get-tuple-element.29.share, bf16[128,1024]{1,0:T(8,128)(2,1)S(1)} %collective-permute-done.refs_1_.refs_0_, ...), custom_call_target="tpu_custom_call" | custom-call | flops 1048576 | bytes 262144 | tf_op jit(solution)/shard_map/whiten_others/pallas_call | solution.py:374
  15.1 2.2 %collective-permute-done.4.refs_1_ = bf16[8,1024]{1,0:T(8,128)(2,1)S(1)} collective-permute-done((bf16[8,1024]{1,0:T(8,128)(2,1)S(1)}, bf16[8,1024]{1,0:T(8,128)(2,1)S(1)}, u32[]{:S(2)}, u32[]{:S(2)}) %collective-permute-start.4) | collective-permute-done | bytes 16416 | tf_op jit(solution)/shard_map/ppermute | solution.py:319
  17.3 1.7 %turn_and_lag.1 = (bf16[2,624,1024]{2,1,0:T(8,128)(2,1)S(1)}, bf16[208,256]{1,0:T(8,128)(2,1)S(1)}, bf16[208,256]{1,0:T(8,128)(2,1)S(1)}, bf16[208,256]{1,0:T(8,128)(2,1)S(1)}) custom-call(bf16[1024,1024]{1,0:T(8,128)(2,1)S(1)} %get-tuple-element.27.table, bf16[512,512]{1,0:T(8,128)(2,1)S(1)} %get-tuple-element.28.weights, ...), custom_call_target="tpu_custom_call" | custom-call | flops 1048576 | bytes 262144 | tf_op jit(solution)/shard_map/turn_and_lag/pallas_call | solution.py:448
  19.0 0.2 collective-permute-start.5
  19.2 1.2 %collective-permute-start.9 = (bf16[208,256]{1,0:T(8,128)(2,1)S(1)}, bf16[208,256]{1,0:T(8,128)(2,1)S(1)}, u32[]{:S(2)}, u32[]{:S(2)}) collective-permute-start(bf16[208,256]{1,0:T(8,128)(2,1)S(1)} %get-tuple-element.37.refs_5_), channel_id=1, source_target_pairs={{12,0},{13,1},{8,4},{9,5},{4,8},{5,9},{0,12},{1,13},{14,2},{15,3},... | collective-permute-start | bytes 319496 | tf_op jit(solution)/shard_map/ppermute | solution.py:319
  20.4 2.2 %collective-permute-start.10 = (bf16[208,256]{1,0:T(8,128)(2,1)S(1)}, bf16[208,256]{1,0:T(8,128)(2,1)S(1)}, u32[]{:S(2)}, u32[]{:S(2)}) collective-permute-start(bf16[208,256]{1,0:T(8,128)(2,1)S(1)} %get-tuple-element.38.refs_6_), channel_id=1, source_target_pairs={{4,0},{5,1},{0,4},{1,5},{12,8},{13,9},{8,12},{9,13},{6,2},{7,3},{2... | collective-permute-start | bytes 319496 | tf_op jit(solution)/shard_map/ppermute | solution.py:319
  22.6 0.8 %lag_base.1.own = f32[624,384]{1,0:T(8,128)S(1)} custom-call(bf16[2,624,1024]{2,1,0:T(8,128)(2,1)S(1)} %get-tuple-element.40.turned, bf16[384,1024]{1,0:T(8,128)(2,1)S(1)} %get-tuple-element.32.own.refs_1_), custom_call_target="tpu_custom_call" | custom-call | flops 1048576 | bytes 262144 | tf_op jit(solution)/shard_map/lag_base/pallas_call | solution.py:462
  23.4 2.5 %collective-permute-done.2.refs_0_ = bf16[384,1024]{1,0:T(8,128)(2,1)S(1)} collective-permute-done((bf16[384,1024]{1,0:T(8,128)(2,1)S(1)}, bf16[384,1024]{1,0:T(8,128)(2,1)S(1)}, u32[]{:S(2)}, u32[]{:S(2)}) %collective-permute-start.2) | collective-permute-done | bytes 786464 | tf_op jit(solution)/shard_map/ppermute | solution.py:331
  25.9 1.7 %whiten_others.3.white.refs_3_ = bf16[1,384,1024]{2,1,0:T(8,128)(2,1)S(1)} custom-call(bf16[1024,1024]{1,0:T(8,128)(2,1)S(1)} %get-tuple-element.27.table, bf16[512,512]{1,0:T(8,128)(2,1)S(1)} %get-tuple-element.28.weights, f32[1,512]{1,0:T(1,128)S(1)} %get-tuple-element.29.share, bf16[384,1024]{1,0:T(8,128)(2,1)S(1)} %collective-permute-done.2.refs_0_), custom_call_target="tpu_custom_call" | custom-call | flops 8589934592 | bytes 67108864 | tf_op jit(solution)/shard_map/whiten_others/pallas_call | solution.py:374
  27.6 0.0 copy-start.1
  27.6 0.9 %lag_pieces.1 = (bf16[208,384]{1,0:T(8,128)(2,1)S(1)}, bf16[208,384]{1,0:T(8,128)(2,1)S(1)}, bf16[208,384]{1,0:T(8,128)(2,1)S(1)}) custom-call(bf16[2,624,1024]{2,1,0:T(8,128)(2,1)S(1)} %get-tuple-element.40.turned, f32[624,384]{1,0:T(8,128)S(1)} %lag_base.1.own, bf16[1,384,1024]{2,1,0:T(8,128)(2,1)S(1)} %whiten_others.3.white.refs_3_, s32[1,384]{1,0:T(1,128)S(1)} %slice.13.mask), custom_call_target="tpu_custom_call" | custom-call | flops 8589934592 | bytes 67108864 | tf_op jit(solution)/shard_map/lag_pieces/pallas_call | solution.py:387
  28.5 0.0 collective-permute-done.5.refs_0_
  28.5 0.1 collective-permute-start.6
  28.6 2.4 %collective-permute-start.7 = (bf16[208,384]{1,0:T(8,128)(2,1)S(1)}, bf16[208,384]{1,0:T(8,128)(2,1)S(1)}, u32[]{:S(2)}, u32[]{:S(2)}) collective-permute-start(bf16[208,384]{1,0:T(8,128)(2,1)S(1)} %get-tuple-element.46.refs_8_), channel_id=1, source_target_pairs={{12,0},{13,1},{8,4},{9,5},{4,8},{5,9},{0,12},{1,13},{14,2},{15,3},... | collective-permute-start | bytes 479240 | tf_op jit(solution)/shard_map/ppermute | solution.py:319
  31.0 1.1 %collective-permute-start.8 = (bf16[208,384]{1,0:T(8,128)(2,1)S(1)}, bf16[208,384]{1,0:T(8,128)(2,1)S(1)}, u32[]{:S(2)}, u32[]{:S(2)}) collective-permute-start(bf16[208,384]{1,0:T(8,128)(2,1)S(1)} %get-tuple-element.47.refs_9_), channel_id=1, source_target_pairs={{4,0},{5,1},{0,4},{1,5},{12,8},{13,9},{8,12},{9,13},{6,2},{7,3},{2... | collective-permute-start | bytes 479240 | tf_op jit(solution)/shard_map/ppermute | solution.py:319
  32.1 0.0 copy-done.1
  32.1 2.8 %receiver_order.1 = (f32[5,101,2,640]{3,2,1,0:T(2,128)}, f32[5,101,2,640]{3,2,1,0:T(2,128)}) custom-call(s32[4,5]{1,0:T(4,128)S(1)} %copy-done.1, bf16[2,208,1024]{2,1,0:T(8,128)(2,1)S(1)} %turn_sources.1.turned, s32[1,640]{1,0:T(1,128)S(1)} %reshape.19.mask, bf16[256,1024]{1,0:T(8,128)(2,1)S(1)} %get-tuple-element.31.own.refs_0_, ...), custom_call_target="tpu_custom_call" | custom-call | flops 8589934592 | bytes 67108864 | tf_op jit(solution)/shard_map/receiver_order/pallas_call | solution.py:487
  35.0 0.0 collective-permute-done.9.refs_1_
  35.0 0.0 collective-permute-done.10.refs_2_
  35.0 1.1 %source_order.2.refs_3_ = f32[5,101,2,640]{3,2,1,0:T(2,128)} custom-call(s32[4,5]{1,0:T(4,128)S(1)} %copy-done.1, bf16[208,256]{1,0:T(8,128)(2,1)S(1)} %collective-permute-done.5.refs_0_, bf16[208,256]{1,0:T(8,128)(2,1)S(1)} %collective-permute-done.9.refs_1_, bf16[208,256]{1,0:T(8,128)(2,1)S(1)} %collective-permute-done.10.refs_2_, ...), custom_call_target="tpu_custom_call", output_to_operand_aliasing={{}: (4, {})} | custom-call | flops 1048576 | bytes 262144 | tf_op jit(solution)/shard_map/source_order/pallas_call | solution.py:499
  36.1 0.3 collective-permute-done.6.refs_0_
  36.4 9.4 %collective-permute-done.7.refs_1_ = bf16[208,384]{1,0:T(8,128)(2,1)S(1)} collective-permute-done((bf16[208,384]{1,0:T(8,128)(2,1)S(1)}, bf16[208,384]{1,0:T(8,128)(2,1)S(1)}, u32[]{:S(2)}, u32[]{:S(2)}) %collective-permute-start.7) | collective-permute-done | bytes 159776 | tf_op jit(solution)/shard_map/ppermute | solution.py:319
  45.8 0.0 collective-permute-done.8.refs_2_
  45.8 1.3 %source_order.3 = f32[5,101,2,640]{3,2,1,0:T(2,128)} custom-call(s32[4,5]{1,0:T(4,128)S(1)} %copy-done.1, bf16[208,384]{1,0:T(8,128)(2,1)S(1)} %collective-permute-done.6.refs_0_, bf16[208,384]{1,0:T(8,128)(2,1)S(1)} %collective-permute-done.7.refs_1_, bf16[208,384]{1,0:T(8,128)(2,1)S(1)} %collective-permute-done.8.refs_2_, ...), custom_call_target="tpu_custom_call", output_to_operand_aliasing={{}: (4, {})} | custom-call | flops 1048576 | bytes 262144 | tf_op jit(solution)/shard_map/source_order/pallas_call | solution.py:499
  (6 shorter events, 0.0 us)
Async XLA Ops:
  1.6 6.5 %copy-start.3 = (s32[640]{0:T(1024)S(1)}, s32[640]{0:T(1024)}, u32[]{:S(2)}) copy-start(s32[640]{0:T(1024)} %param.8) | copy-start | bytes 7684
  1.6 7.3 %copy-start.2 = (s32[4]{0:T(128)S(1)}, s32[4]{0:T(128)}, u32[]{:S(2)}) copy-start(s32[4]{0:T(128)} %phases.1) | copy-start | bytes 52
  1.6 7.2 %collective-permute-start = (bf16[128,1024]{1,0:T(8,128)(2,1)S(1)}, bf16[128,1024]{1,0:T(8,128)(2,1)S(1)}, u32[]{:S(2)}, u32[]{:S(2)}) collective-permute-start(bf16[128,1024]{1,0:T(8,128)(2,1)S(1)} %bitcast.7), channel_id=1, source_target_pairs={{0,2},{2,0},{1,3},{3,1},{4,6},{6,4},{5,7},{7,5},{8,10},{10,8},{9,1... | collective-permute-start | bytes 786440 | tf_op jit(solution)/shard_map/ppermute | solution.py:331
  2.9 9.8 %copy-start = (f32[104,1024]{1,0:T(8,128)S(1)}, f32[104,1024]{1,0:T(8,128)}, u32[]{:S(2)}) copy-start(f32[104,1024]{1,0:T(8,128)} %constant.13.clone.lags) | copy-start | bytes 1277956
  7.8 18.2 %collective-permute-start.2 = (bf16[384,1024]{1,0:T(8,128)(2,1)S(1)}, bf16[384,1024]{1,0:T(8,128)(2,1)S(1)}, u32[]{:S(2)}, u32[]{:S(2)}) collective-permute-start(bf16[384,1024]{1,0:T(8,128)(2,1)S(1)} %slice.9), channel_id=1, source_target_pairs={{0,2},{2,0},{1,3},{3,1},{4,6},{6,4},{5,7},{7,5},{8,10},{10,8},{9,1... | collective-permute-start | bytes 2359304 | tf_op jit(solution)/shard_map/ppermute | solution.py:331
  9.6 4.1 %collective-permute-start.3 = (f32[4,1024]{1,0:T(4,128)S(1)}, f32[4,1024]{1,0:T(4,128)S(1)}, u32[]{:S(2)}, u32[]{:S(2)}) collective-permute-start(f32[4,1024]{1,0:T(4,128)S(1)} %pick_sources.1.refs_0_), channel_id=1, source_target_pairs={{4,0},{5,1},{0,4},{1,5},{12,8},{13,9},{8,12},{9,13},{6,2},{7,3},{2... | collective-permute-start | bytes 49160 | tf_op jit(solution)/shard_map/ppermute | solution.py:319
  10.9 3.0 %collective-permute-start.1 = (bf16[128,1024]{1,0:T(8,128)(2,1)S(1)}, bf16[128,1024]{1,0:T(8,128)(2,1)S(1)}, u32[]{:S(2)}, u32[]{:S(2)}) collective-permute-start(bf16[128,1024]{1,0:T(8,128)(2,1)S(1)} %collective-permute-done.refs_1_.refs_0_), channel_id=1, source_target_pairs={{0,1},{1,0},{2,3},{3,2},{4,5},{5,4},{6,7},{7,6},{8,9},{9,8},{10,11... | collective-permute-start | bytes 786440 | tf_op jit(solution)/shard_map/ppermute | solution.py:331
  13.7 3.6 %collective-permute-start.4 = (bf16[8,1024]{1,0:T(8,128)(2,1)S(1)}, bf16[8,1024]{1,0:T(8,128)(2,1)S(1)}, u32[]{:S(2)}, u32[]{:S(2)}) collective-permute-start(bf16[8,1024]{1,0:T(8,128)(2,1)S(1)} %pad_maximum_fusion), channel_id=1, source_target_pairs={{8,0},{9,1},{12,4},{13,5},{0,8},{1,9},{4,12},{5,13},{10,2},{11,3},... | collective-permute-start | bytes 49160 | tf_op jit(solution)/shard_map/ppermute | solution.py:319
  19.0 9.5 %collective-permute-start.5 = (bf16[208,256]{1,0:T(8,128)(2,1)S(1)}, bf16[208,256]{1,0:T(8,128)(2,1)S(1)}, u32[]{:S(2)}, u32[]{:S(2)}) collective-permute-start(bf16[208,256]{1,0:T(8,128)(2,1)S(1)} %get-tuple-element.36.refs_4_), channel_id=1, source_target_pairs={{8,0},{9,1},{12,4},{13,5},{0,8},{1,9},{4,12},{5,13},{10,2},{11,3},... | collective-permute-start | bytes 319496 | tf_op jit(solution)/shard_map/ppermute | solution.py:319
  19.2 15.8 %collective-permute-start.9 = (bf16[208,256]{1,0:T(8,128)(2,1)S(1)}, bf16[208,256]{1,0:T(8,128)(2,1)S(1)}, u32[]{:S(2)}, u32[]{:S(2)}) collective-permute-start(bf16[208,256]{1,0:T(8,128)(2,1)S(1)} %get-tuple-element.37.refs_5_), channel_id=1, source_target_pairs={{12,0},{13,1},{8,4},{9,5},{4,8},{5,9},{0,12},{1,13},{14,2},{15,3},... | collective-permute-start | bytes 319496 | tf_op jit(solution)/shard_map/ppermute | solution.py:319
  20.4 14.6 %collective-permute-start.10 = (bf16[208,256]{1,0:T(8,128)(2,1)S(1)}, bf16[208,256]{1,0:T(8,128)(2,1)S(1)}, u32[]{:S(2)}, u32[]{:S(2)}) collective-permute-start(bf16[208,256]{1,0:T(8,128)(2,1)S(1)} %get-tuple-element.38.refs_6_), channel_id=1, source_target_pairs={{4,0},{5,1},{0,4},{1,5},{12,8},{13,9},{8,12},{9,13},{6,2},{7,3},{2... | collective-permute-start | bytes 319496 | tf_op jit(solution)/shard_map/ppermute | solution.py:319
  27.6 4.5 %copy-start.1 = (s32[4,5]{1,0:T(4,128)S(1)}, s32[4,5]{1,0:T(4,128)}, u32[]{:S(2)}) copy-start(s32[4,5]{1,0:T(4,128)} %pairs.5) | copy-start | bytes 244
  28.5 7.9 %collective-permute-start.6 = (bf16[208,384]{1,0:T(8,128)(2,1)S(1)}, bf16[208,384]{1,0:T(8,128)(2,1)S(1)}, u32[]{:S(2)}, u32[]{:S(2)}) collective-permute-start(bf16[208,384]{1,0:T(8,128)(2,1)S(1)} %get-tuple-element.45.refs_7_), channel_id=1, source_target_pairs={{8,0},{9,1},{12,4},{13,5},{0,8},{1,9},{4,12},{5,13},{10,2},{11,3},... | collective-permute-start | bytes 479240 | tf_op jit(solution)/shard_map/ppermute | solution.py:319
  28.6 17.2 %collective-permute-start.7 = (bf16[208,384]{1,0:T(8,128)(2,1)S(1)}, bf16[208,384]{1,0:T(8,128)(2,1)S(1)}, u32[]{:S(2)}, u32[]{:S(2)}) collective-permute-start(bf16[208,384]{1,0:T(8,128)(2,1)S(1)} %get-tuple-element.46.refs_8_), channel_id=1, source_target_pairs={{12,0},{13,1},{8,4},{9,5},{4,8},{5,9},{0,12},{1,13},{14,2},{15,3},... | collective-permute-start | bytes 479240 | tf_op jit(solution)/shard_map/ppermute | solution.py:319
  31.0 14.7 %collective-permute-start.8 = (bf16[208,384]{1,0:T(8,128)(2,1)S(1)}, bf16[208,384]{1,0:T(8,128)(2,1)S(1)}, u32[]{:S(2)}, u32[]{:S(2)}) collective-permute-start(bf16[208,384]{1,0:T(8,128)(2,1)S(1)} %get-tuple-element.47.refs_9_), channel_id=1, source_target_pairs={{4,0},{5,1},{0,4},{1,5},{12,8},{13,9},{8,12},{9,13},{6,2},{7,3},{2... | collective-permute-start | bytes 479240 | tf_op jit(solution)/shard_map/ppermute | solution.py:319
where the time goes:
time: 47.2 us; the launch traced here: 47.1 us
  Pallas kernels  17.9 us (38%)
  waiting for transfers between devices  15.2 us (32%)
  starting transfers between devices  12.1 us (26%)
  local copies, waits for them, and re-layouts  1.06 us (2%)
  between operations  0.8 us (2%)
    ppermute x8, waiting for transfers between devices, exchange(): return lax.ppermute(value, ('chan', 'sub'), route)  11.9 us
    ppermute x8, starting transfers between devices, exchange(): return lax.ppermute(value, ('chan', 'sub'), route)  8.68 us
    pallas_call x1, Pallas kernels, on_device(): pl.pallas_call(functools.partial(setup_kernel, chunks), out_shape=tuple((...  4.79 us
    ppermute x3, starting transfers between devices, shift(): lax.ppermute(block, axis, [(i, (i + distance) % count) for i in range(cou...  3.42 us
    ppermute x3, waiting for transfers between devices, shift(): lax.ppermute(block, axis, [(i, (i + distance) % count) for i in range(cou...  3.32 us
    pallas_call x2, Pallas kernels, whiten_others(): pl.pallas_call(others_kernel, out_shape=like((windows - 1, size, 2 * NB),...  2.89 us
    pallas_call x1, Pallas kernels, on_device(): pl.pallas_call(functools.partial(receiver_kernel, (ties, blocks, per_devi...  2.83 us
    pallas_call x2, Pallas kernels, on_device(): pl.pallas_call(functools.partial(source_kernel, (ties[1:], blocks, per_de...  2.4 us
  transfers between devices with their start and end apart: 11, of which 5 were waited for; matrix products, arithmetic and copies ran while one was open for 0% of the time, Pallas kernels for 35%

commit v1 on v0

--- a/solution.py
+++ b/solution.py
@@ -183,9 +183,12 @@
             for half, place in ((parts[2 * i], sub_at), (parts[2 * i + 1], 1 - sub_at)):
                 raw[:, pl.ds(place, 1)] = half[...].reshape(groups, 1, group, samples)
             rows = raw[...].reshape(white.shape[1], samples)
-        real, imag = whiten(rows, table[...], weights[...], share[...])
-        white[i, :, :NB] = real
-        white[i, :, NB:] = imag
+        block = rows.shape[0] // 2 if rows.shape[0] % 32 == 0 else rows.shape[0]
+        for start in range(0, rows.shape[0], block):
+            span = slice(start, start + block)
+            real, imag = whiten(rows[span], table[...], weights[...], share[...])
+            white[i, span, :NB] = real
+            white[i, span, NB:] = imag
 
 
 def lag_product(turned, own, white):

time: 47.2 us -> 47.4 us (level)
  transfers between devices with their start and end apart: 11 -> 11, of which waited for: 5 -> 5; matrix products, arithmetic and copies ran while one was open for 0% -> 0% of each run, Pallas kernels for 35% -> 36%
where the time goes in v1:
time: 47.4 us; the launch traced here: 47.2 us
  Pallas kernels  18.2 us (38%)
  waiting for transfers between devices  15 us (32%)
  starting transfers between devices  12.1 us (26%)
  local copies, waits for them, and re-layouts  1.06 us (2%)
  between operations  0.8 us (2%)
    ppermute x8, waiting for transfers between devices, exchange(): return lax.ppermute(value, ('chan', 'sub'), route)  11.7 us
    ppermute x8, starting transfers between devices, exchange(): return lax.ppermute(value, ('chan', 'sub'), route)  8.68 us
    pallas_call x1, Pallas kernels, on_device(): pl.pallas_call(functools.partial(setup_kernel, chunks), out_shape=tuple((...  4.79 us
    ppermute x3, starting transfers between devices, shift(): lax.ppermute(block, axis, [(i, (i + distance) % count) for i in range(cou...  3.42 us
    ppermute x3, waiting for transfers between devices, shift(): lax.ppermute(block, axis, [(i, (i + distance) % count) for i in range(cou...  3.32 us
    pallas_call x2, Pallas kernels, whiten_others(): pl.pallas_call(others_kernel, out_shape=like((windows - 1, size, 2 * NB),...  3.23 us
    pallas_call x1, Pallas kernels, on_device(): pl.pallas_call(functools.partial(receiver_kernel, (ties, blocks, per_devi...  2.83 us
    pallas_call x2, Pallas kernels, on_device(): pl.pallas_call(functools.partial(source_kernel, (ties[1:], blocks, per_de...  2.4 us
  transfers between devices with their start and end apart: 11, of which 5 were waited for; matrix products, arithmetic and copies ran while one was open for 0% of the time, Pallas kernels for 36%

profile of v1, /device:TPU:17, one launch (start us, length us, event | category | flops | bytes accessed | tf_op | source)
XLA Modules:
  0.0 47.2 jit_solution(6503735173822459951)
XLA Ops:
  0.6 1.0 %constant_dynamic-slice_fusion = bf16[8,1,16,1024]{3,2,1,0:T(8,128)(2,1)S(1)} fusion(bf16[20,2,16,1024]{3,2,1,0:T(8,128)(2,1)} %bitcast.10, s32[]{:T(128)S(6)} %select_n.3), kind=kLoop, calls=%fused_computation.1 | loop fusion | bytes 524292 | tf_op jit(solution)/shard_map/dynamic_slice | solution.py:367
  1.6 0.0 copy-start.3
  1.6 0.0 copy-start.2
  1.6 1.3 %collective-permute-start = (bf16[128,1024]{1,0:T(8,128)(2,1)S(1)}, bf16[128,1024]{1,0:T(8,128)(2,1)S(1)}, u32[]{:S(2)}, u32[]{:S(2)}) collective-permute-start(bf16[128,1024]{1,0:T(8,128)(2,1)S(1)} %bitcast.7), channel_id=1, source_target_pairs={{0,2},{2,0},{1,3},{3,1},{4,6},{6,4},{5,7},{7,5},{8,10},{10,8},{9,1... | collective-permute-start | bytes 786440 | tf_op jit(solution)/shard_map/ppermute | solution.py:334
  2.9 0.0 copy-start
  2.9 4.8 %whiten_own.1 = (bf16[256,1024]{1,0:T(8,128)(2,1)S(1)}, bf16[384,1024]{1,0:T(8,128)(2,1)S(1)}, bf16[512,512]{1,0:T(8,128)(2,1)S(1)}, f32[1,512]{1,0:T(1,128)S(1)...) custom-call(bf16[1,640,1024]{2,1,0:T(8,128)(2,1)} %traces.1, bf16[1024,1024]{1,0:T(8,128)(2,1)} %constant.12.clone.table, ...), custom_call_target="tpu_custom_call" | custom-call | flops 1048576 | bytes 262144 | tf_op jit(solution)/shard_map/whiten_own/pallas_call | solution.py:402
  7.7 0.1 slice.9
  7.8 0.3 collective-permute-start.2
  8.1 0.0 copy-done.3
  8.1 0.8 %collective-permute-done.refs_1_.refs_0_ = bf16[128,1024]{1,0:T(8,128)(2,1)S(1)} collective-permute-done((bf16[128,1024]{1,0:T(8,128)(2,1)S(1)}, bf16[128,1024]{1,0:T(8,128)(2,1)S(1)}, u32[]{:S(2)}, u32[]{:S(2)}) %collective-permute-start) | collective-permute-done | bytes 262176 | tf_op jit(solution)/shard_map/ppermute | solution.py:334
  8.9 0.0 copy-done.2
  8.9 0.7 %pick_sources.1.refs_0_ = f32[4,1024]{1,0:T(4,128)S(1)} custom-call(s32[4]{0:T(128)S(1)} %copy-done.2, s32[1,640]{1,0:T(1,128)S(1)} %reshape.19.mask, bf16[128,1024]{1,0:T(8,128)(2,1)S(1)} %bitcast.8, bf16[128,1024]{1,0:T(8,128)(2,1)S(1)} %collective-permute-done.refs_1_.refs_0_), custom_call_target="tpu_custom_call" | custom-call | flops 1048576 | bytes 262144 | tf_op jit(solution)/shard_map/pick_sources/pallas_call | solution.py:415
  9.6 1.3 %collective-permute-start.3 = (f32[4,1024]{1,0:T(4,128)S(1)}, f32[4,1024]{1,0:T(4,128)S(1)}, u32[]{:S(2)}, u32[]{:S(2)}) collective-permute-start(f32[4,1024]{1,0:T(4,128)S(1)} %pick_sources.1.refs_0_), channel_id=1, source_target_pairs={{4,0},{5,1},{0,4},{1,5},{12,8},{13,9},{8,12},{9,13},{6,2},{7,3},{2... | collective-permute-start | bytes 49160 | tf_op jit(solution)/shard_map/ppermute | solution.py:322
  10.9 1.8 %collective-permute-start.1 = (bf16[128,1024]{1,0:T(8,128)(2,1)S(1)}, bf16[128,1024]{1,0:T(8,128)(2,1)S(1)}, u32[]{:S(2)}, u32[]{:S(2)}) collective-permute-start(bf16[128,1024]{1,0:T(8,128)(2,1)S(1)} %collective-permute-done.refs_1_.refs_0_), channel_id=1, source_target_pairs={{0,1},{1,0},{2,3},{3,2},{4,5},{5,4},{6,7},{7,6},{8,9},{9,8},{10,11... | collective-permute-start | bytes 786440 | tf_op jit(solution)/shard_map/ppermute | solution.py:334
  12.7 0.0 copy-done
  12.7 0.9 %turn_sources.1.turned = bf16[2,208,1024]{2,1,0:T(8,128)(2,1)S(1)} custom-call(bf16[1024,1024]{1,0:T(8,128)(2,1)S(1)} %get-tuple-element.27.table, bf16[512,512]{1,0:T(8,128)(2,1)S(1)} %get-tuple-element.28.weights, f32[1,512]{1,0:T(1,128)S(1)} %get-tuple-element.29.share, f32[104,1024]{1,0:T(8,128)S(1)} %copy-done, f32[4,1024]{1,0:T(4,128)S(1)} %pick_sources.1.refs_0_), custom_call_target="tpu_custom_call" | custom-call | flops 8589934592 | bytes 67108864 | tf_op jit(solution)/shard_map/turn_sources/pallas_call | solution.py:427
  13.7 0.0 collective-permute-done.3.refs_0_
  13.7 0.1 collective-permute-start.4
  13.9 0.0 collective-permute-done.1.refs_1_
  13.9 1.4 %whiten_others.2.white.refs_2_ = bf16[1,256,1024]{2,1,0:T(8,128)(2,1)S(1)} custom-call(bf16[1024,1024]{1,0:T(8,128)(2,1)S(1)} %get-tuple-element.27.table, bf16[512,512]{1,0:T(8,128)(2,1)S(1)} %get-tuple-element.28.weights, f32[1,512]{1,0:T(1,128)S(1)} %get-tuple-element.29.share, bf16[128,1024]{1,0:T(8,128)(2,1)S(1)} %collective-permute-done.refs_1_.refs_0_, ...), custom_call_target="tpu_custom_call" | custom-call | flops 1048576 | bytes 262144 | tf_op jit(solution)/shard_map/whiten_others/pallas_call | solution.py:377
  15.3 2.0 %collective-permute-done.4.refs_1_ = bf16[8,1024]{1,0:T(8,128)(2,1)S(1)} collective-permute-done((bf16[8,1024]{1,0:T(8,128)(2,1)S(1)}, bf16[8,1024]{1,0:T(8,128)(2,1)S(1)}, u32[]{:S(2)}, u32[]{:S(2)}) %collective-permute-start.4) | collective-permute-done | bytes 16416 | tf_op jit(solution)/shard_map/ppermute | solution.py:322
  17.3 1.7 %turn_and_lag.1 = (bf16[2,624,1024]{2,1,0:T(8,128)(2,1)S(1)}, bf16[208,256]{1,0:T(8,128)(2,1)S(1)}, bf16[208,256]{1,0:T(8,128)(2,1)S(1)}, bf16[208,256]{1,0:T(8,128)(2,1)S(1)}) custom-call(bf16[1024,1024]{1,0:T(8,128)(2,1)S(1)} %get-tuple-element.27.table, bf16[512,512]{1,0:T(8,128)(2,1)S(1)} %get-tuple-element.28.weights, ...), custom_call_target="tpu_custom_call" | custom-call | flops 1048576 | bytes 262144 | tf_op jit(solution)/shard_map/turn_and_lag/pallas_call | solution.py:451
  19.0 0.4 collective-permute-start.5
  19.3 1.0 %collective-permute-start.9 = (bf16[208,256]{1,0:T(8,128)(2,1)S(1)}, bf16[208,256]{1,0:T(8,128)(2,1)S(1)}, u32[]{:S(2)}, u32[]{:S(2)}) collective-permute-start(bf16[208,256]{1,0:T(8,128)(2,1)S(1)} %get-tuple-element.37.refs_5_), channel_id=1, source_target_pairs={{12,0},{13,1},{8,4},{9,5},{4,8},{5,9},{0,12},{1,13},{14,2},{15,3},... | collective-permute-start | bytes 319496 | tf_op jit(solution)/shard_map/ppermute | solution.py:322
  20.4 2.2 %collective-permute-start.10 = (bf16[208,256]{1,0:T(8,128)(2,1)S(1)}, bf16[208,256]{1,0:T(8,128)(2,1)S(1)}, u32[]{:S(2)}, u32[]{:S(2)}) collective-permute-start(bf16[208,256]{1,0:T(8,128)(2,1)S(1)} %get-tuple-element.38.refs_6_), channel_id=1, source_target_pairs={{4,0},{5,1},{0,4},{1,5},{12,8},{13,9},{8,12},{9,13},{6,2},{7,3},{2... | collective-permute-start | bytes 319496 | tf_op jit(solution)/shard_map/ppermute | solution.py:322
  22.6 0.8 %lag_base.1.own = f32[624,384]{1,0:T(8,128)S(1)} custom-call(bf16[2,624,1024]{2,1,0:T(8,128)(2,1)S(1)} %get-tuple-element.40.turned, bf16[384,1024]{1,0:T(8,128)(2,1)S(1)} %get-tuple-element.32.own.refs_1_), custom_call_target="tpu_custom_call" | custom-call | flops 1048576 | bytes 262144 | tf_op jit(solution)/shard_map/lag_base/pallas_call | solution.py:465
  23.4 2.5 %collective-permute-done.2.refs_0_ = bf16[384,1024]{1,0:T(8,128)(2,1)S(1)} collective-permute-done((bf16[384,1024]{1,0:T(8,128)(2,1)S(1)}, bf16[384,1024]{1,0:T(8,128)(2,1)S(1)}, u32[]{:S(2)}, u32[]{:S(2)}) %collective-permute-start.2) | collective-permute-done | bytes 786464 | tf_op jit(solution)/shard_map/ppermute | solution.py:334
  25.9 1.8 %whiten_others.3.white.refs_3_ = bf16[1,384,1024]{2,1,0:T(8,128)(2,1)S(1)} custom-call(bf16[1024,1024]{1,0:T(8,128)(2,1)S(1)} %get-tuple-element.27.table, bf16[512,512]{1,0:T(8,128)(2,1)S(1)} %get-tuple-element.28.weights, f32[1,512]{1,0:T(1,128)S(1)} %get-tuple-element.29.share, bf16[384,1024]{1,0:T(8,128)(2,1)S(1)} %collective-permute-done.2.refs_0_), custom_call_target="tpu_custom_call" | custom-call | flops 8589934592 | bytes 67108864 | tf_op jit(solution)/shard_map/whiten_others/pallas_call | solution.py:377
  27.8 0.0 copy-start.1
  27.8 0.9 %lag_pieces.1 = (bf16[208,384]{1,0:T(8,128)(2,1)S(1)}, bf16[208,384]{1,0:T(8,128)(2,1)S(1)}, bf16[208,384]{1,0:T(8,128)(2,1)S(1)}) custom-call(bf16[2,624,1024]{2,1,0:T(8,128)(2,1)S(1)} %get-tuple-element.40.turned, f32[624,384]{1,0:T(8,128)S(1)} %lag_base.1.own, bf16[1,384,1024]{2,1,0:T(8,128)(2,1)S(1)} %whiten_others.3.white.refs_3_, s32[1,384]{1,0:T(1,128)S(1)} %slice.13.mask), custom_call_target="tpu_custom_call" | custom-call | flops 8589934592 | bytes 67108864 | tf_op jit(solution)/shard_map/lag_pieces/pallas_call | solution.py:390
  28.7 0.0 collective-permute-done.5.refs_0_
  28.7 0.1 collective-permute-start.6
  28.8 2.4 %collective-permute-start.7 = (bf16[208,384]{1,0:T(8,128)(2,1)S(1)}, bf16[208,384]{1,0:T(8,128)(2,1)S(1)}, u32[]{:S(2)}, u32[]{:S(2)}) collective-permute-start(bf16[208,384]{1,0:T(8,128)(2,1)S(1)} %get-tuple-element.46.refs_8_), channel_id=1, source_target_pairs={{12,0},{13,1},{8,4},{9,5},{4,8},{5,9},{0,12},{1,13},{14,2},{15,3},... | collective-permute-start | bytes 479240 | tf_op jit(solution)/shard_map/ppermute | solution.py:322
  31.2 1.1 %collective-permute-start.8 = (bf16[208,384]{1,0:T(8,128)(2,1)S(1)}, bf16[208,384]{1,0:T(8,128)(2,1)S(1)}, u32[]{:S(2)}, u32[]{:S(2)}) collective-permute-start(bf16[208,384]{1,0:T(8,128)(2,1)S(1)} %get-tuple-element.47.refs_9_), channel_id=1, source_target_pairs={{4,0},{5,1},{0,4},{1,5},{12,8},{13,9},{8,12},{9,13},{6,2},{7,3},{2... | collective-permute-start | bytes 479240 | tf_op jit(solution)/shard_map/ppermute | solution.py:322
  32.3 0.0 copy-done.1
  32.3 2.8 %receiver_order.1 = (f32[5,101,2,640]{3,2,1,0:T(2,128)}, f32[5,101,2,640]{3,2,1,0:T(2,128)}) custom-call(s32[4,5]{1,0:T(4,128)S(1)} %copy-done.1, bf16[2,208,1024]{2,1,0:T(8,128)(2,1)S(1)} %turn_sources.1.turned, s32[1,640]{1,0:T(1,128)S(1)} %reshape.19.mask, bf16[256,1024]{1,0:T(8,128)(2,1)S(1)} %get-tuple-element.31.own.refs_0_, ...), custom_call_target="tpu_custom_call" | custom-call | flops 8589934592 | bytes 67108864 | tf_op jit(solution)/shard_map/receiver_order/pallas_call | solution.py:490
  35.1 0.0 collective-permute-done.9.refs_1_
  35.1 0.0 collective-permute-done.10.refs_2_
  35.1 1.1 %source_order.2.refs_3_ = f32[5,101,2,640]{3,2,1,0:T(2,128)} custom-call(s32[4,5]{1,0:T(4,128)S(1)} %copy-done.1, bf16[208,256]{1,0:T(8,128)(2,1)S(1)} %collective-permute-done.5.refs_0_, bf16[208,256]{1,0:T(8,128)(2,1)S(1)} %collective-permute-done.9.refs_1_, bf16[208,256]{1,0:T(8,128)(2,1)S(1)} %collective-permute-done.10.refs_2_, ...), custom_call_target="tpu_custom_call", output_to_operand_aliasing={{}: (4, {})} | custom-call | flops 1048576 | bytes 262144 | tf_op jit(solution)/shard_map/source_order/pallas_call | solution.py:502
  36.3 0.3 collective-permute-done.6.refs_0_
  36.6 9.4 %collective-permute-done.7.refs_1_ = bf16[208,384]{1,0:T(8,128)(2,1)S(1)} collective-permute-done((bf16[208,384]{1,0:T(8,128)(2,1)S(1)}, bf16[208,384]{1,0:T(8,128)(2,1)S(1)}, u32[]{:S(2)}, u32[]{:S(2)}) %collective-permute-start.7) | collective-permute-done | bytes 159776 | tf_op jit(solution)/shard_map/ppermute | solution.py:322
  45.9 0.0 collective-permute-done.8.refs_2_
  45.9 1.3 %source_order.3 = f32[5,101,2,640]{3,2,1,0:T(2,128)} custom-call(s32[4,5]{1,0:T(4,128)S(1)} %copy-done.1, bf16[208,384]{1,0:T(8,128)(2,1)S(1)} %collective-permute-done.6.refs_0_, bf16[208,384]{1,0:T(8,128)(2,1)S(1)} %collective-permute-done.7.refs_1_, bf16[208,384]{1,0:T(8,128)(2,1)S(1)} %collective-permute-done.8.refs_2_, ...), custom_call_target="tpu_custom_call", output_to_operand_aliasing={{}: (4, {})} | custom-call | flops 1048576 | bytes 262144 | tf_op jit(solution)/shard_map/source_order/pallas_call | solution.py:502
  (6 shorter events, 0.0 us)
Async XLA Ops:
  1.6 6.5 %copy-start.3 = (s32[640]{0:T(1024)S(1)}, s32[640]{0:T(1024)}, u32[]{:S(2)}) copy-start(s32[640]{0:T(1024)} %param.8) | copy-start | bytes 7684
  1.6 7.3 %copy-start.2 = (s32[4]{0:T(128)S(1)}, s32[4]{0:T(128)}, u32[]{:S(2)}) copy-start(s32[4]{0:T(128)} %phases.1) | copy-start | bytes 52
  1.6 7.2 %collective-permute-start = (bf16[128,1024]{1,0:T(8,128)(2,1)S(1)}, bf16[128,1024]{1,0:T(8,128)(2,1)S(1)}, u32[]{:S(2)}, u32[]{:S(2)}) collective-permute-start(bf16[128,1024]{1,0:T(8,128)(2,1)S(1)} %bitcast.7), channel_id=1, source_target_pairs={{0,2},{2,0},{1,3},{3,1},{4,6},{6,4},{5,7},{7,5},{8,10},{10,8},{9,1... | collective-permute-start | bytes 786440 | tf_op jit(solution)/shard_map/ppermute | solution.py:334
  2.9 9.8 %copy-start = (f32[104,1024]{1,0:T(8,128)S(1)}, f32[104,1024]{1,0:T(8,128)}, u32[]{:S(2)}) copy-start(f32[104,1024]{1,0:T(8,128)} %constant.13.clone.lags) | copy-start | bytes 1277956
  7.8 18.2 %collective-permute-start.2 = (bf16[384,1024]{1,0:T(8,128)(2,1)S(1)}, bf16[384,1024]{1,0:T(8,128)(2,1)S(1)}, u32[]{:S(2)}, u32[]{:S(2)}) collective-permute-start(bf16[384,1024]{1,0:T(8,128)(2,1)S(1)} %slice.9), channel_id=1, source_target_pairs={{0,2},{2,0},{1,3},{3,1},{4,6},{6,4},{5,7},{7,5},{8,10},{10,8},{9,1... | collective-permute-start | bytes 2359304 | tf_op jit(solution)/shard_map/ppermute | solution.py:334
  9.6 4.1 %collective-permute-start.3 = (f32[4,1024]{1,0:T(4,128)S(1)}, f32[4,1024]{1,0:T(4,128)S(1)}, u32[]{:S(2)}, u32[]{:S(2)}) collective-permute-start(f32[4,1024]{1,0:T(4,128)S(1)} %pick_sources.1.refs_0_), channel_id=1, source_target_pairs={{4,0},{5,1},{0,4},{1,5},{12,8},{13,9},{8,12},{9,13},{6,2},{7,3},{2... | collective-permute-start | bytes 49160 | tf_op jit(solution)/shard_map/ppermute | solution.py:322
  10.9 3.0 %collective-permute-start.1 = (bf16[128,1024]{1,0:T(8,128)(2,1)S(1)}, bf16[128,1024]{1,0:T(8,128)(2,1)S(1)}, u32[]{:S(2)}, u32[]{:S(2)}) collective-permute-start(bf16[128,1024]{1,0:T(8,128)(2,1)S(1)} %collective-permute-done.refs_1_.refs_0_), channel_id=1, source_target_pairs={{0,1},{1,0},{2,3},{3,2},{4,5},{5,4},{6,7},{7,6},{8,9},{9,8},{10,11... | collective-permute-start | bytes 786440 | tf_op jit(solution)/shard_map/ppermute | solution.py:334
  13.7 3.6 %collective-permute-start.4 = (bf16[8,1024]{1,0:T(8,128)(2,1)S(1)}, bf16[8,1024]{1,0:T(8,128)(2,1)S(1)}, u32[]{:S(2)}, u32[]{:S(2)}) collective-permute-start(bf16[8,1024]{1,0:T(8,128)(2,1)S(1)} %pad_maximum_fusion), channel_id=1, source_target_pairs={{8,0},{9,1},{12,4},{13,5},{0,8},{1,9},{4,12},{5,13},{10,2},{11,3},... | collective-permute-start | bytes 49160 | tf_op jit(solution)/shard_map/ppermute | solution.py:322
  19.0 9.7 %collective-permute-start.5 = (bf16[208,256]{1,0:T(8,128)(2,1)S(1)}, bf16[208,256]{1,0:T(8,128)(2,1)S(1)}, u32[]{:S(2)}, u32[]{:S(2)}) collective-permute-start(bf16[208,256]{1,0:T(8,128)(2,1)S(1)} %get-tuple-element.36.refs_4_), channel_id=1, source_target_pairs={{8,0},{9,1},{12,4},{13,5},{0,8},{1,9},{4,12},{5,13},{10,2},{11,3},... | collective-permute-start | bytes 319496 | tf_op jit(solution)/shard_map/ppermute | solution.py:322
  19.3 15.8 %collective-permute-start.9 = (bf16[208,256]{1,0:T(8,128)(2,1)S(1)}, bf16[208,256]{1,0:T(8,128)(2,1)S(1)}, u32[]{:S(2)}, u32[]{:S(2)}) collective-permute-start(bf16[208,256]{1,0:T(8,128)(2,1)S(1)} %get-tuple-element.37.refs_5_), channel_id=1, source_target_pairs={{12,0},{13,1},{8,4},{9,5},{4,8},{5,9},{0,12},{1,13},{14,2},{15,3},... | collective-permute-start | bytes 319496 | tf_op jit(solution)/shard_map/ppermute | solution.py:322
  20.4 14.8 %collective-permute-start.10 = (bf16[208,256]{1,0:T(8,128)(2,1)S(1)}, bf16[208,256]{1,0:T(8,128)(2,1)S(1)}, u32[]{:S(2)}, u32[]{:S(2)}) collective-permute-start(bf16[208,256]{1,0:T(8,128)(2,1)S(1)} %get-tuple-element.38.refs_6_), channel_id=1, source_target_pairs={{4,0},{5,1},{0,4},{1,5},{12,8},{13,9},{8,12},{9,13},{6,2},{7,3},{2... | collective-permute-start | bytes 319496 | tf_op jit(solution)/shard_map/ppermute | solution.py:322
  27.8 4.5 %copy-start.1 = (s32[4,5]{1,0:T(4,128)S(1)}, s32[4,5]{1,0:T(4,128)}, u32[]{:S(2)}) copy-start(s32[4,5]{1,0:T(4,128)} %pairs.5) | copy-start | bytes 244
  28.7 7.9 %collective-permute-start.6 = (bf16[208,384]{1,0:T(8,128)(2,1)S(1)}, bf16[208,384]{1,0:T(8,128)(2,1)S(1)}, u32[]{:S(2)}, u32[]{:S(2)}) collective-permute-start(bf16[208,384]{1,0:T(8,128)(2,1)S(1)} %get-tuple-element.45.refs_7_), channel_id=1, source_target_pairs={{8,0},{9,1},{12,4},{13,5},{0,8},{1,9},{4,12},{5,13},{10,2},{11,3},... | collective-permute-start | bytes 479240 | tf_op jit(solution)/shard_map/ppermute | solution.py:322
  28.8 17.2 %collective-permute-start.7 = (bf16[208,384]{1,0:T(8,128)(2,1)S(1)}, bf16[208,384]{1,0:T(8,128)(2,1)S(1)}, u32[]{:S(2)}, u32[]{:S(2)}) collective-permute-start(bf16[208,384]{1,0:T(8,128)(2,1)S(1)} %get-tuple-element.46.refs_8_), channel_id=1, source_target_pairs={{12,0},{13,1},{8,4},{9,5},{4,8},{5,9},{0,12},{1,13},{14,2},{15,3},... | collective-permute-start | bytes 479240 | tf_op jit(solution)/shard_map/ppermute | solution.py:322
  31.2 14.8 %collective-permute-start.8 = (bf16[208,384]{1,0:T(8,128)(2,1)S(1)}, bf16[208,384]{1,0:T(8,128)(2,1)S(1)}, u32[]{:S(2)}, u32[]{:S(2)}) collective-permute-start(bf16[208,384]{1,0:T(8,128)(2,1)S(1)} %get-tuple-element.47.refs_9_), channel_id=1, source_target_pairs={{4,0},{5,1},{0,4},{1,5},{12,8},{13,9},{8,12},{9,13},{6,2},{7,3},{2... | collective-permute-start | bytes 479240 | tf_op jit(solution)/shard_map/ppermute | solution.py:322
